TPU v7x, 512 devices: a whole 4x8x8 slice. The times are simulated.
512 devices in a mesh: frame: 16 (over x, z_lo), height: 16 (over y, core), cand: 2 (over z_hi).
Axes of the slice: x: 4, y: 8, z: 8 (z_hi: 2, z_lo: 4; z = z_hi * 4 + z_lo), core: 2. Of those that a mesh axis runs over, the one named last changes fastest.
Arguments:
- queries: bfloat16 [64, 64, 16, 1536], P(('cand', 'frame'), 'height'), parts along dimension 0, may hold values from -6 to 6
- key_value: bfloat16 [2, 64, 64, 16, 1536], P(None, ('cand', 'frame'), 'height'), parts along dimension 1, may hold values from -6 to 6
- windows: int32 [12, 3], replicated, may hold values from 0 to 1, as said below
Outputs:
- attended: bfloat16 [64, 64, 16, 1536], P(('cand', 'frame'), 'height'), parts along dimension 0
There are 2 independent parts, one for each index of `cand`. A program takes and returns all parts, laid end to end along the dimension named above; an argument that names none is the same for every part. Nothing has to cross between parts.
Inputs may be any that keep to these rules, and one draw needn't show every extreme that they name: `windows`: column 0 is at most 1, column 1 at most 1, column 2 at most 1; each column reaches its most for some head and 0 for another.
All inputs are finite; a program needn't handle non-finite values.
Results may differ from a plain program's by a relative error of at most 0.0046.
Values may be sent and summed in bfloat16 or wider, within the bound.
A program may use at most 64 MiB of HBM per device.

v0:
```python
import math

import jax
import jax.numpy as jnp
from jax import lax
from jax.sharding import PartitionSpec as P

TF = 2
TH = 8
TW = 8
WF_MAX = 1
WH_MAX = 1


def from_behind(block, axis, distance):
    devices = range(lax.axis_size(axis))
    route = [(i - distance, i) for i in devices if i - distance in devices]
    return lax.ppermute(block, axis, route)


def positions(frame_start, frame_count, row_start, row_count, columns):
    grid_shape = (frame_count, row_count, columns)
    frame_ids = frame_start + lax.broadcasted_iota(jnp.int32, grid_shape, 0)
    row_ids = row_start + lax.broadcasted_iota(jnp.int32, grid_shape, 1)
    column_ids = lax.broadcasted_iota(jnp.int32, grid_shape, 2)
    return (frame_ids.reshape(-1), row_ids.reshape(-1), column_ids.reshape(-1))


def within(key_pos, frames_all, rows_all):
    return (
        (key_pos[0] >= 0) & (key_pos[0] < frames_all) & (key_pos[1] >= 0) & (key_pos[1] < rows_all)
    )


def tile_distances(query_pos, key_pos):
    result = []
    for dimension, extent in enumerate((TF, TH, TW)):
        result.append(
            jnp.abs(query_pos[dimension][:, None] // extent - key_pos[dimension][None, :] // extent)
        )
    return result


def attend_head(query_cols, key_cols, value_cols, distances, inside_grid, window_row):
    scaling = 1.0 / math.sqrt(query_cols.shape[-1])
    scores = (
        lax.dot_general(
            query_cols, key_cols, (((1,), (1,)), ((), ())), preferred_element_type=jnp.float32
        )
        * scaling
    )
    permitted = (
        inside_grid[None, :]
        & (distances[0] <= window_row[0])
        & (distances[1] <= window_row[1])
        & (distances[2] <= window_row[2])
    )
    masked = jnp.where(permitted, scores, -jnp.inf)
    largest = jnp.max(masked, axis=-1, keepdims=True)
    exponentials = jnp.exp(masked - largest)
    totals = jnp.sum(exponentials, axis=-1)
    weights = exponentials.astype(jnp.bfloat16)
    blended = jnp.dot(weights, value_cols, preferred_element_type=jnp.float32)
    return (blended / totals[:, None]).astype(jnp.bfloat16)


def shards(queries, key_value, windows):
    frame_count, row_count, columns, width_all = queries.shape
    head_count = windows.shape[0]
    head_size = width_all // head_count
    frames_all = frame_count * lax.axis_size("frame")
    rows_all = row_count * lax.axis_size("height")
    frame_start = lax.axis_index("frame") * frame_count
    row_start = lax.axis_index("height") * row_count
    frame_margin = WF_MAX * TF + TF - frame_count
    row_margin = WH_MAX * TH + TH - row_count
    frame_steps = frame_margin // frame_count
    row_steps = row_margin // row_count
    key_frames = (2 * WF_MAX + 1) * TF
    key_rows = (2 * WH_MAX + 1) * TH
    key_frame_start = frame_start // TF * TF - WF_MAX * TF
    key_row_start = row_start // TH * TH - WH_MAX * TH
    frame_offset = key_frame_start - (frame_start - frame_margin)
    row_offset = key_row_start - (row_start - row_margin)
    pieces = []
    for step in range(frame_steps, -frame_steps - 1, -1):
        if step == 0:
            pieces.append(key_value)
        else:
            pieces.append(from_behind(key_value, "frame", step))
    framed = jnp.concatenate(pieces, axis=1)
    pieces = []
    for step in range(row_steps, -row_steps - 1, -1):
        if step == 0:
            pieces.append(framed)
        else:
            pieces.append(from_behind(framed, "height", step))
    extended = lax.dynamic_slice_in_dim(jnp.concatenate(pieces, axis=2), row_offset, key_rows, 2)
    query_pos = positions(frame_start, frame_count, row_start, row_count, columns)
    key_pos = positions(key_frame_start, key_frames, key_row_start, key_rows, columns)
    inside_grid = within(key_pos, frames_all, rows_all)
    distances = tile_distances(query_pos, key_pos)
    flat_queries = queries.reshape(-1, width_all)
    flat_keys = extended[0].reshape(-1, width_all)
    flat_values = extended[1].reshape(-1, width_all)
    results = []
    for head in range(head_count):
        first = head * head_size
        last = first + head_size
        results.append(
            attend_head(
                flat_queries[:, first:last],
                flat_keys[:, first:last],
                flat_values[:, first:last],
                distances,
                inside_grid,
                windows[head],
            )
        )
    return jnp.concatenate(results, axis=1).reshape(queries.shape)


def solution(mesh):
    in_specs = (
        P(("cand", "frame"), "height", None, None),
        P(None, ("cand", "frame"), "height", None, None),
        P(),
    )
    out_specs = P(("cand", "frame"), "height", None, None)
    return jax.shard_map(shards, mesh=mesh, in_specs=in_specs, out_specs=out_specs, check_vma=False)
```

profile of v0, /device:TPU:1, one launch (start us, length us, event | category | flops | bytes accessed | tf_op | source)
XLA Modules:
  0.0 287.7 jit_solution(11357520235168087458)
XLA Ops:
  0.0 5.0 %collective-permute-start = (bf16[2,2,4,16,1536]{4,3,2,1,0:T(8,128)(2,1)}, bf16[2,2,4,16,1536]{4,3,2,1,0:T(8,128)(2,1)S(1)}, u32[]{:S(2)}, u32[]{:S(2)}) collective-permute-start(bf16[2,2,4,16,1536]{4,3,2,1,0:T(8,128)(2,1)} %param.4), channel_id=1, source_target_pairs={{0,32},{32,64},{64,96},{96,128},{128,160},{160,192},{192,224},{224... | collective-permute-start | bytes 2359304 | tf_op jit(solution)/shard_map/ppermute | solution.py:18
  5.0 1.3 collective-permute-start.1
  6.3 12.7 %collective-permute-done = bf16[2,2,4,16,1536]{4,3,2,1,0:T(8,128)(2,1)S(1)} collective-permute-done((bf16[2,2,4,16,1536]{4,3,2,1,0:T(8,128)(2,1)}, bf16[2,2,4,16,1536]{4,3,2,1,0:T(8,128)(2,1)S(1)}, u32[]{:S(2)}, u32[]{:S(2)}) %collective-permute-start) | collective-permute-done | bytes 786464 | tf_op jit(solution)/shard_map/ppermute | solution.py:18
  19.0 1.0 constant_dynamic-update-slice_fusion.2
  20.0 1.0 constant_dynamic-update-slice_fusion.1
  21.0 22.6 %collective-permute-done.1 = bf16[2,2,4,16,1536]{4,3,2,1,0:T(8,128)(2,1)S(1)} collective-permute-done((bf16[2,2,4,16,1536]{4,3,2,1,0:T(8,128)(2,1)}, bf16[2,2,4,16,1536]{4,3,2,1,0:T(8,128)(2,1)S(1)}, u32[]{:S(2)}, u32[]{:S(2)}) %collective-permute-start.1) | collective-permute-done | bytes 786464 | tf_op jit(solution)/shard_map/ppermute | solution.py:18
  43.5 1.0 constant_dynamic-update-slice_fusion
  44.5 6.1 %collective-permute-start.2 = (bf16[2,6,4,16,1536]{4,3,2,1,0:T(8,128)(2,1)}, bf16[2,6,4,16,1536]{4,3,2,1,0:T(8,128)(2,1)}, u32[]{:S(2)}, u32[]{:S(2)}) collective-permute-start(bf16[2,6,4,16,1536]{4,3,2,1,0:T(8,128)(2,1)} %constant_dynamic-update-slice_fusion), channel_id=1, source_target_pairs={{0,6},{2,8},{4,10},{6,12},{8,14},{10,16},{12,18},{14,20},{16,22},{... | collective-permute-start | bytes 7077896 | tf_op jit(solution)/shard_map/ppermute | solution.py:18
  50.6 3.2 %collective-permute-start.3 = (bf16[2,6,4,16,1536]{4,3,2,1,0:T(8,128)(2,1)}, bf16[2,6,4,16,1536]{4,3,2,1,0:T(8,128)(2,1)}, u32[]{:S(2)}, u32[]{:S(2)}) collective-permute-start(bf16[2,6,4,16,1536]{4,3,2,1,0:T(8,128)(2,1)} %constant_dynamic-update-slice_fusion), channel_id=1, source_target_pairs={{0,4},{2,6},{4,8},{6,10},{8,12},{10,14},{12,16},{14,18},{16,20},{1... | collective-permute-start | bytes 7077896 | tf_op jit(solution)/shard_map/ppermute | solution.py:18
  53.9 1.9 collective-permute-start.4
  56.1 0.1 reshape.483
  56.4 3.8 %collective-permute-start.5 = (bf16[2,6,4,16,1536]{4,3,2,1,0:T(8,128)(2,1)}, bf16[2,6,4,16,1536]{4,3,2,1,0:T(8,128)(2,1)}, u32[]{:S(2)}, u32[]{:S(2)}) collective-permute-start(bf16[2,6,4,16,1536]{4,3,2,1,0:T(8,128)(2,1)} %constant_dynamic-update-slice_fusion), channel_id=1, source_target_pairs={{2,0},{4,2},{6,4},{8,6},{10,8},{12,10},{14,12},{16,14},{18,16},{20... | collective-permute-start | bytes 7077896 | tf_op jit(solution)/shard_map/ppermute | solution.py:18
  60.4 1.3 collective-permute-start.6
  61.7 0.7 fusion.210
  62.6 37.9 %collective-permute-done.2 = bf16[2,6,4,16,1536]{4,3,2,1,0:T(8,128)(2,1)} collective-permute-done((bf16[2,6,4,16,1536]{4,3,2,1,0:T(8,128)(2,1)}, bf16[2,6,4,16,1536]{4,3,2,1,0:T(8,128)(2,1)}, u32[]{:S(2)}, u32[]{:S(2)}) %collective-permute-start.2) | collective-permute-done | bytes 2359328 | tf_op jit(solution)/shard_map/ppermute | solution.py:18
  100.5 1.3 collective-permute-start.7
  101.8 0.7 fusion.211
  102.5 1.8 constant_dynamic-update-slice_fusion.11
  104.4 45.9 %collective-permute-done.3 = bf16[2,6,4,16,1536]{4,3,2,1,0:T(8,128)(2,1)} collective-permute-done((bf16[2,6,4,16,1536]{4,3,2,1,0:T(8,128)(2,1)}, bf16[2,6,4,16,1536]{4,3,2,1,0:T(8,128)(2,1)}, u32[]{:S(2)}, u32[]{:S(2)}) %collective-permute-start.3) | collective-permute-done | bytes 2359328 | tf_op jit(solution)/shard_map/ppermute | solution.py:18
  150.3 1.8 constant_dynamic-update-slice_fusion.10
  152.1 23.5 %collective-permute-done.4 = bf16[2,6,4,16,1536]{4,3,2,1,0:T(8,128)(2,1)} collective-permute-done((bf16[2,6,4,16,1536]{4,3,2,1,0:T(8,128)(2,1)}, bf16[2,6,4,16,1536]{4,3,2,1,0:T(8,128)(2,1)}, u32[]{:S(2)}, u32[]{:S(2)}) %collective-permute-start.4) | collective-permute-done | bytes 2359328 | tf_op jit(solution)/shard_map/ppermute | solution.py:18
  175.6 1.8 constant_dynamic-update-slice_fusion.9
  177.6 1.8 constant_dynamic-update-slice_fusion.5
  179.4 1.8 constant_dynamic-update-slice_fusion.4
  181.2 33.2 %collective-permute-done.7 = bf16[2,6,4,16,1536]{4,3,2,1,0:T(8,128)(2,1)S(1)} collective-permute-done((bf16[2,6,4,16,1536]{4,3,2,1,0:T(8,128)(2,1)}, bf16[2,6,4,16,1536]{4,3,2,1,0:T(8,128)(2,1)S(1)}, u32[]{:S(2)}, u32[]{:S(2)}) %collective-permute-start.7) | collective-permute-done | bytes 2359328 | tf_op jit(solution)/shard_map/ppermute | solution.py:18
  214.5 0.2 constant_dynamic-update-slice_fusion.3
  214.6 1.2 constant_dynamic-slice_fusion.1
  215.9 3.3 %fusion.212 = (f32[128]{0:T(128)S(1)}, f32[128,2304]{0,1:T(8,128)S(1)}) fusion(bf16[128,1536]{1,0:T(8,128)(2,1)S(1)} %bitcast.118, bf16[2304,1536]{1,0:T(8,128)(2,1)S(1)} %bitcast.100, s32[]{:T(128)} %bitcast.2, s32[2304]{0:T(1024)S(1)} %get-tuple-element.69, s32[128]{0:T(128)S(1)} %get-tuple-element.67, s32[]{:T(128)} %bitcast.1, ...), kind=kOutput, calls=%fused_computation.285 | convolution fusion | flops 79921024 | bytes 1844236 | tf_op jit(solution)/shard_map/dot_general | solution.py:47
  219.2 0.3 fusion.120
  219.5 0.4 fusion.97
  219.9 3.2 %fusion.213 = (f32[128]{0:T(128)S(1)}, f32[128,2304]{0,1:T(8,128)S(1)}) fusion(bf16[128,1536]{1,0:T(8,128)(2,1)S(1)} %bitcast.119, bf16[2304,1536]{1,0:T(8,128)(2,1)S(1)} %bitcast.101, s32[]{:T(128)} %bitcast.9, s32[2304]{0:T(1024)S(1)} %get-tuple-element.69, s32[128]{0:T(128)S(1)} %get-tuple-element.67, s32[]{:T(128)} %bitcast.8, ...), kind=kOutput, calls=%fused_computation.286 | convolution fusion | flops 79921024 | bytes 1844236 | tf_op jit(solution)/shard_map/dot_general | solution.py:47
  223.1 0.3 fusion.122
  223.5 0.4 fusion.99
  223.9 3.1 %fusion.214 = (f32[128]{0:T(128)S(1)}, f32[128,2304]{0,1:T(8,128)S(1)}) fusion(bf16[128,1536]{1,0:T(8,128)(2,1)S(1)} %bitcast.120, bf16[2304,1536]{1,0:T(8,128)(2,1)S(1)} %bitcast.102, s32[]{:T(128)} %bitcast.13, s32[2304]{0:T(1024)S(1)} %get-tuple-element.69, s32[128]{0:T(128)S(1)} %get-tuple-element.67, s32[]{:T(128)} %bitcast.12, ...), kind=kOutput, calls=%fused_computation.287 | convolution fusion | flops 79921024 | bytes 1844236 | tf_op jit(solution)/shard_map/dot_general | solution.py:47
  227.0 0.3 fusion.124
  227.4 0.4 fusion.101
  227.8 3.3 %fusion.215 = (f32[128]{0:T(128)S(1)}, f32[128,2304]{0,1:T(8,128)S(1)}) fusion(bf16[128,1536]{1,0:T(8,128)(2,1)S(1)} %bitcast.121, bf16[2304,1536]{1,0:T(8,128)(2,1)S(1)} %bitcast.103, s32[]{:T(128)} %bitcast.17, s32[2304]{0:T(1024)S(1)} %get-tuple-element.69, s32[128]{0:T(128)S(1)} %get-tuple-element.67, s32[]{:T(128)} %bitcast.16, ...), kind=kOutput, calls=%fused_computation.288 | convolution fusion | flops 79921024 | bytes 1844236 | tf_op jit(solution)/shard_map/dot_general | solution.py:47
  231.1 0.3 fusion.126
  231.4 0.4 fusion.103
  231.9 3.3 %fusion.216 = (f32[128]{0:T(128)S(1)}, f32[128,2304]{0,1:T(8,128)S(1)}) fusion(bf16[128,1536]{1,0:T(8,128)(2,1)S(1)} %bitcast.122, bf16[2304,1536]{1,0:T(8,128)(2,1)S(1)} %bitcast.104, s32[]{:T(128)} %bitcast.21, s32[2304]{0:T(1024)S(1)} %get-tuple-element.69, s32[128]{0:T(128)S(1)} %get-tuple-element.67, s32[]{:T(128)} %bitcast.20, ...), kind=kOutput, calls=%fused_computation.289 | convolution fusion | flops 79921024 | bytes 1844236 | tf_op jit(solution)/shard_map/dot_general | solution.py:47
  235.1 0.3 fusion.128
  235.5 1.5 fusion.105
  237.0 5.4 %fusion.217 = (f32[128]{0:T(128)S(1)}, f32[128,2304]{0,1:T(8,128)S(1)}) fusion(bf16[128,1536]{1,0:T(8,128)(2,1)} %bitcast.112, bf16[2304,1536]{1,0:T(8,128)(2,1)} %bitcast.105, s32[]{:T(128)} %bitcast.25, s32[2304]{0:T(1024)S(1)} %get-tuple-element.69, s32[128]{0:T(128)S(1)} %get-tuple-element.67, s32[]{:T(128)} %bitcast.24, ...), kind=kOutput, calls=%fused_computation.290 | convolution fusion | flops 79921024 | bytes 1835776 | tf_op jit(solution)/shard_map/dot_general | solution.py:47
  242.3 0.3 fusion.130
  242.7 1.5 fusion.107
  244.2 5.4 %fusion.218 = (f32[128]{0:T(128)S(1)}, f32[128,2304]{0,1:T(8,128)S(1)}) fusion(bf16[128,1536]{1,0:T(8,128)(2,1)} %bitcast.113, bf16[2304,1536]{1,0:T(8,128)(2,1)} %bitcast.106, s32[]{:T(128)} %bitcast.29, s32[2304]{0:T(1024)S(1)} %get-tuple-element.69, s32[128]{0:T(128)S(1)} %get-tuple-element.67, s32[]{:T(128)} %bitcast.28, ...), kind=kOutput, calls=%fused_computation.291 | convolution fusion | flops 79921024 | bytes 1835776 | tf_op jit(solution)/shard_map/dot_general | solution.py:47
  249.6 0.3 fusion.132
  249.9 1.5 fusion.109
  251.4 5.3 %fusion.219 = (f32[128]{0:T(128)S(1)}, f32[128,2304]{0,1:T(8,128)S(1)}) fusion(bf16[128,1536]{1,0:T(8,128)(2,1)} %bitcast.114, bf16[2304,1536]{1,0:T(8,128)(2,1)} %bitcast.107, s32[]{:T(128)} %bitcast.33, s32[2304]{0:T(1024)S(1)} %get-tuple-element.69, s32[128]{0:T(128)S(1)} %get-tuple-element.67, s32[]{:T(128)} %bitcast.32, ...), kind=kOutput, calls=%fused_computation.292 | convolution fusion | flops 79921024 | bytes 1835776 | tf_op jit(solution)/shard_map/dot_general | solution.py:47
  256.7 0.3 fusion.134
  257.0 1.5 fusion.111
  258.5 5.3 %fusion.220 = (f32[128]{0:T(128)S(1)}, f32[128,2304]{0,1:T(8,128)S(1)}) fusion(bf16[128,1536]{1,0:T(8,128)(2,1)} %bitcast.115, bf16[2304,1536]{1,0:T(8,128)(2,1)} %bitcast.108, s32[]{:T(128)} %bitcast.37, s32[2304]{0:T(1024)S(1)} %get-tuple-element.69, s32[128]{0:T(128)S(1)} %get-tuple-element.67, s32[]{:T(128)} %bitcast.36, ...), kind=kOutput, calls=%fused_computation.293 | convolution fusion | flops 79921024 | bytes 1835776 | tf_op jit(solution)/shard_map/dot_general | solution.py:47
  263.8 0.3 fusion.136
  264.1 1.5 fusion.113
  265.6 5.2 %fusion.221 = (f32[128]{0:T(128)S(1)}, f32[128,2304]{0,1:T(8,128)S(1)}) fusion(bf16[128,1536]{1,0:T(8,128)(2,1)} %bitcast.116, bf16[2304,1536]{1,0:T(8,128)(2,1)} %bitcast.109, s32[]{:T(128)} %bitcast.41, s32[2304]{0:T(1024)S(1)} %get-tuple-element.69, s32[128]{0:T(128)S(1)} %get-tuple-element.67, s32[]{:T(128)} %bitcast.40, ...), kind=kOutput, calls=%fused_computation.294 | convolution fusion | flops 79921024 | bytes 1835776 | tf_op jit(solution)/shard_map/dot_general | solution.py:47
  270.8 0.3 fusion.138
  271.2 1.5 fusion.115
  272.6 5.2 %fusion.222 = (f32[128]{0:T(128)S(1)}, f32[128,2304]{0,1:T(8,128)S(1)}) fusion(bf16[128,1536]{1,0:T(8,128)(2,1)} %bitcast.117, bf16[2304,1536]{1,0:T(8,128)(2,1)} %bitcast.110, s32[]{:T(128)} %bitcast.45, s32[2304]{0:T(1024)S(1)} %get-tuple-element.69, s32[128]{0:T(128)S(1)} %get-tuple-element.67, s32[]{:T(128)} %bitcast.44, ...), kind=kOutput, calls=%fused_computation.295 | convolution fusion | flops 79921024 | bytes 1835776 | tf_op jit(solution)/shard_map/dot_general | solution.py:47
  277.8 0.3 fusion.140
  278.2 1.5 fusion.117
  279.7 5.3 %fusion.223 = (f32[128]{0:T(128)S(1)}, f32[128,2304]{0,1:T(8,128)S(1)}) fusion(bf16[128,1536]{1,0:T(8,128)(2,1)S(1)} %bitcast.123, bf16[2304,1536]{1,0:T(8,128)(2,1)} %bitcast.111, s32[]{:T(128)} %bitcast.49, s32[2304]{0:T(1024)S(1)} %get-tuple-element.69, s32[128]{0:T(128)S(1)} %get-tuple-element.67, s32[]{:T(128)} %bitcast.48, ...), kind=kOutput, calls=%fused_computation.296 | convolution fusion | flops 79921024 | bytes 1845760 | tf_op jit(solution)/shard_map/dot_general | solution.py:47
  284.9 0.3 fusion.142
  285.3 1.5 fusion.119
  286.8 0.9 copy.5
  (35 shorter events, 1.0 us)
Async XLA Ops:
  0.0 20.0 %copy-start.2 = (bf16[2,2,4,16,1536]{4,3,2,1,0:T(8,128)(2,1)S(1)}, bf16[2,2,4,16,1536]{4,3,2,1,0:T(8,128)(2,1)}, u32[]{:S(2)}) copy-start(bf16[2,2,4,16,1536]{4,3,2,1,0:T(8,128)(2,1)} %param.4) | copy-start | bytes 2359300
  0.0 19.0 %collective-permute-start = (bf16[2,2,4,16,1536]{4,3,2,1,0:T(8,128)(2,1)}, bf16[2,2,4,16,1536]{4,3,2,1,0:T(8,128)(2,1)S(1)}, u32[]{:S(2)}, u32[]{:S(2)}) collective-permute-start(bf16[2,2,4,16,1536]{4,3,2,1,0:T(8,128)(2,1)} %param.4), channel_id=1, source_target_pairs={{0,32},{32,64},{64,96},{96,128},{128,160},{160,192},{192,224},{224... | collective-permute-start | bytes 2359304 | tf_op jit(solution)/shard_map/ppermute | solution.py:18
  5.0 38.5 %collective-permute-start.1 = (bf16[2,2,4,16,1536]{4,3,2,1,0:T(8,128)(2,1)}, bf16[2,2,4,16,1536]{4,3,2,1,0:T(8,128)(2,1)S(1)}, u32[]{:S(2)}, u32[]{:S(2)}) collective-permute-start(bf16[2,2,4,16,1536]{4,3,2,1,0:T(8,128)(2,1)} %param.4), channel_id=1, source_target_pairs={{32,0},{64,32},{96,64},{128,96},{160,128},{192,160},{224,192},{256... | collective-permute-start | bytes 2359304 | tf_op jit(solution)/shard_map/ppermute | solution.py:18
  21.0 40.7 %copy-start.3 = (s32[12,3]{0,1:T(4,128)S(1)}, s32[12,3]{0,1:T(4,128)}, u32[]{:S(2)}) copy-start(s32[12,3]{0,1:T(4,128)} %param.5) | copy-start | bytes 436
  44.5 56.0 %collective-permute-start.2 = (bf16[2,6,4,16,1536]{4,3,2,1,0:T(8,128)(2,1)}, bf16[2,6,4,16,1536]{4,3,2,1,0:T(8,128)(2,1)}, u32[]{:S(2)}, u32[]{:S(2)}) collective-permute-start(bf16[2,6,4,16,1536]{4,3,2,1,0:T(8,128)(2,1)} %constant_dynamic-update-slice_fusion), channel_id=1, source_target_pairs={{0,6},{2,8},{4,10},{6,12},{8,14},{10,16},{12,18},{14,20},{16,22},{... | collective-permute-start | bytes 7077896 | tf_op jit(solution)/shard_map/ppermute | solution.py:18
  50.6 99.7 %collective-permute-start.3 = (bf16[2,6,4,16,1536]{4,3,2,1,0:T(8,128)(2,1)}, bf16[2,6,4,16,1536]{4,3,2,1,0:T(8,128)(2,1)}, u32[]{:S(2)}, u32[]{:S(2)}) collective-permute-start(bf16[2,6,4,16,1536]{4,3,2,1,0:T(8,128)(2,1)} %constant_dynamic-update-slice_fusion), channel_id=1, source_target_pairs={{0,4},{2,6},{4,8},{6,10},{8,12},{10,14},{12,16},{14,18},{16,20},{1... | collective-permute-start | bytes 7077896 | tf_op jit(solution)/shard_map/ppermute | solution.py:18
  53.9 121.7 %collective-permute-start.4 = (bf16[2,6,4,16,1536]{4,3,2,1,0:T(8,128)(2,1)}, bf16[2,6,4,16,1536]{4,3,2,1,0:T(8,128)(2,1)}, u32[]{:S(2)}, u32[]{:S(2)}) collective-permute-start(bf16[2,6,4,16,1536]{4,3,2,1,0:T(8,128)(2,1)} %constant_dynamic-update-slice_fusion), channel_id=1, source_target_pairs={{0,2},{2,4},{4,6},{6,8},{8,10},{10,12},{12,14},{14,16},{16,18},{18... | collective-permute-start | bytes 7077896 | tf_op jit(solution)/shard_map/ppermute | solution.py:18
  56.4 121.2 %collective-permute-start.5 = (bf16[2,6,4,16,1536]{4,3,2,1,0:T(8,128)(2,1)}, bf16[2,6,4,16,1536]{4,3,2,1,0:T(8,128)(2,1)}, u32[]{:S(2)}, u32[]{:S(2)}) collective-permute-start(bf16[2,6,4,16,1536]{4,3,2,1,0:T(8,128)(2,1)} %constant_dynamic-update-slice_fusion), channel_id=1, source_target_pairs={{2,0},{4,2},{6,4},{8,6},{10,8},{12,10},{14,12},{16,14},{18,16},{20... | collective-permute-start | bytes 7077896 | tf_op jit(solution)/shard_map/ppermute | solution.py:18
  60.4 119.0 %collective-permute-start.6 = (bf16[2,6,4,16,1536]{4,3,2,1,0:T(8,128)(2,1)}, bf16[2,6,4,16,1536]{4,3,2,1,0:T(8,128)(2,1)}, u32[]{:S(2)}, u32[]{:S(2)}) collective-permute-start(bf16[2,6,4,16,1536]{4,3,2,1,0:T(8,128)(2,1)} %constant_dynamic-update-slice_fusion), channel_id=1, source_target_pairs={{4,0},{6,2},{8,4},{10,6},{12,8},{14,10},{16,12},{18,14},{20,16},{2... | collective-permute-start | bytes 7077896 | tf_op jit(solution)/shard_map/ppermute | solution.py:18
  100.5 113.9 %collective-permute-start.7 = (bf16[2,6,4,16,1536]{4,3,2,1,0:T(8,128)(2,1)}, bf16[2,6,4,16,1536]{4,3,2,1,0:T(8,128)(2,1)S(1)}, u32[]{:S(2)}, u32[]{:S(2)}) collective-permute-start(bf16[2,6,4,16,1536]{4,3,2,1,0:T(8,128)(2,1)} %constant_dynamic-update-slice_fusion), channel_id=1, source_target_pairs={{6,0},{8,2},{10,4},{12,6},{14,8},{16,10},{18,12},{20,14},{22,16},{... | collective-permute-start | bytes 7077896 | tf_op jit(solution)/shard_map/ppermute | solution.py:18
  214.6 1.3 copy-start.4
  215.9 15.6 %copy-start = (bf16[1,6,24,16,1536]{4,3,2,1,0:T(8,128)(2,1)}, bf16[1,6,24,16,1536]{4,3,2,1,0:T(8,128)(2,1)S(1)}, u32[]{:S(2)}) copy-start(bf16[1,6,24,16,1536]{4,3,2,1,0:T(8,128)(2,1)S(1)} %get-tuple-element.5) | copy-start | bytes 21233668
  215.9 16.0 %copy-start.1 = (bf16[1,6,24,16,1536]{4,3,2,1,0:T(8,128)(2,1)}, bf16[1,6,24,16,1536]{4,3,2,1,0:T(8,128)(2,1)S(1)}, u32[]{:S(2)}) copy-start(bf16[1,6,24,16,1536]{4,3,2,1,0:T(8,128)(2,1)S(1)} %get-tuple-element.6) | copy-start | bytes 21233668
where the time goes:
time: 289 us; the launch traced here: 288 us
  waiting for transfers between devices  176 us (61%)
  matrix products  66.8 us (23%)
  starting transfers between devices  23.9 us (8%)
  local copies, waits for them, and re-layouts  16.8 us (6%)
  other arithmetic  4.04 us (1%)
    ppermute x8, waiting for transfers between devices, from_behind(): return lax.ppermute(block, axis, route)  176 us
    dot_general x12, matrix products, attend_head(): lax.dot_general(query_cols, key_cols, (((1,), (1,)), ((), ())), preferred...  53.2 us
    ppermute x8, starting transfers between devices, from_behind(): return lax.ppermute(block, axis, route)  23.9 us
    dot_general x12, matrix products, attend_head(): blended = jnp.dot(weights, value_cols, preferred_element_type=jnp.float32)  13.6 us
    unnamed x20, local copies, waits for them, and re-layouts  11.2 us
  transfers between devices with their start and end apart: 8, of which 6 were waited for; matrix products, arithmetic and copies ran while one was open for 5% of the time, Pallas kernels for 0%

commit v1 on v0

v1 whole, which is shorter than its diff:
```python
import functools
import math

import jax
import jax.numpy as jnp
from jax import lax
from jax.experimental import pallas as pl
from jax.experimental.pallas import tpu as pltpu
from jax.sharding import PartitionSpec as P

HEADS = 12
HALF = HEADS // 2
HD = 128
TOK = 128
CHIP = 2 * TOK
W = 16
TW = 8
NEG = -1e30
SCALE = math.log2(math.e) / math.sqrt(HD)
MESH = pl.DeviceIdType.MESH


def dot(a, b, dims):
    return lax.dot_general(a, b, ((dims[0], dims[1]), ((), ())), preferred_element_type=jnp.float32)


PLANS = ((4, 0, 12), (5, 0, 12), (6, 0, 12), (7, 0, 12), (8, 0, 12), (12, 0, 12))


def sort_kernel(q, kv, win, packed, flags, choice):
    keys, tall, wide, lone = [], jnp.int32(0), jnp.int32(0), jnp.int32(0)
    for h in range(HEADS):
        wf, wh = jnp.minimum(win[h, 0], 1), jnp.minimum(win[h, 1], 1)
        keys.append((3 - 3 * wf - wh + 2 * wf * wh) * 16 + h)
        wide = wide + wf
        tall = tall + wh
        lone = lone + wf * (1 - wh)
    ranks = []
    for h in range(HEADS):
        rank = jnp.int32(0)
        for k in range(HEADS):
            if k != h:
                rank = rank + jnp.where(keys[k] < keys[h], 1, 0)
        ranks.append(rank)
    for s in range(HEADS):
        head = jnp.int32(0)
        for h in range(HEADS):
            head = head + jnp.where(ranks[h] == s, h, 0)
        for i in range(3):
            flags[s, i] = win[head, i]
        flags[s, 3] = ranks[s]
        col = pl.multiple_of(head * HD, HD)
        packed[s, 0] = kv[0, :, pl.ds(col, HD)]
        packed[s, 1] = kv[1, :, pl.ds(col, HD)].T
        packed[s, 2] = q[:, pl.ds(col, HD)]
    best = jnp.int32(len(PLANS) - 1)
    for i in reversed(range(len(PLANS) - 1)):
        nf, h0, h1 = PLANS[i]
        best = jnp.where((wide <= nf) & (lone >= h0) & (lone + tall <= h1), i, best)
    choice[0] = best


def place_kernel(o, flags, out):
    for h in range(HEADS):
        out[:, h * HD : (h + 1) * HD] = o[flags[h, 3]]


def kernel(
    cfg,
    n_frame,
    n_chip_y,
    packed,
    flags,
    out,
    own,
    nb,
    qn,
    acc,
    ml,
    rs,
    rr,
    oh,
    own_l,
    own_s,
    own_r,
    z_s,
    z_r,
    q_s,
    q_r,
    ret_s,
    ret_r,
    o_l,
    o_s,
    o_r,
):
    nf, h0, h1 = cfg
    f = lax.axis_index("frame")
    height = lax.axis_index("height")
    y = height // 2
    c = height % 2
    other = 1 - c
    z_ok = (f > 0, f < n_frame - 1)
    y_ok = (y > 0, y < n_chip_y - 1)
    z_dev = (f - 1, f + 1)
    y_dev = (y - 1, y + 1)
    partner = {"height": 2 * y + other}

    barrier = pltpu.get_barrier_semaphore()
    pl.semaphore_signal(barrier, inc=1, device_id=partner, device_id_type=MESH)
    for d in range(2):

        @pl.when(z_ok[d])
        def _():
            for g in range(2):
                pl.semaphore_signal(
                    barrier,
                    inc=1,
                    device_id={"frame": z_dev[d], "height": 2 * y + g},
                    device_id_type=MESH,
                )

        @pl.when(y_ok[d])
        def _():
            for g in range(2):
                pl.semaphore_signal(
                    barrier,
                    inc=1,
                    device_id={"height": 2 * y_dev[d] + g},
                    device_id_type=MESH,
                )

    def own_load(j):
        return pltpu.make_async_copy(packed.at[2 * j + c], own.at[j, c], own_l.at[j])

    @pl.loop(0, HALF)
    def _(j):
        own_load(j).start()

    for d in range(2):

        @pl.when(jnp.logical_not(y_ok[d]))
        def _():
            rr[d] = jnp.zeros(rr.shape[1:], rr.dtype)

    pl.semaphore_wait(
        barrier,
        1
        + 2 * sum(jnp.where(ok, 1, 0) for ok in z_ok)
        + 2 * sum(jnp.where(ok, 1, 0) for ok in y_ok),
    )

    def z_copy(d, j, mine):
        g = c if mine else other
        return pltpu.make_async_remote_copy(
            src_ref=packed.at[2 * j + g, pl.ds(0, 2)],
            dst_ref=nb.at[1 - d, j, c],
            send_sem=z_s.at[d, j, 0 if mine else 1],
            recv_sem=z_r.at[1 - d, j, c],
            device_id={"frame": z_dev[d], "height": 2 * y + g},
            device_id_type=MESH,
        )

    def q_copy(d, j, mine):
        g = c if mine else other
        return pltpu.make_async_remote_copy(
            src_ref=packed.at[2 * j + g, 2],
            dst_ref=qn.at[1 - d, j, c],
            send_sem=q_s.at[d, j, 0 if mine else 1],
            recv_sem=q_r.at[1 - d, j, c],
            device_id={"height": 2 * y_dev[d] + g},
            device_id_type=MESH,
        )

    def own_copy(j):
        return pltpu.make_async_remote_copy(
            src_ref=packed.at[2 * j + other],
            dst_ref=own.at[j, c],
            send_sem=own_s.at[j],
            recv_sem=own_r.at[j],
            device_id=partner,
            device_id_type=MESH,
        )

    def ret_copy(d, j):
        return pltpu.make_async_remote_copy(
            src_ref=rs.at[d, j],
            dst_ref=rr.at[1 - d, j],
            send_sem=ret_s.at[d, j],
            recv_sem=ret_r.at[1 - d, j],
            device_id={"height": 2 * y_dev[d] + c},
            device_id_type=MESH,
        )

    def o_copy(j):
        return pltpu.make_async_remote_copy(
            src_ref=oh.at[j, other],
            dst_ref=out.at[2 * j + c],
            send_sem=o_s.at[j],
            recv_sem=o_r.at[j],
            device_id=partner,
            device_id_type=MESH,
        )

    def o_store(j):
        return pltpu.make_async_copy(oh.at[j, c], out.at[2 * j + c], o_l.at[j])

    def z_count(g):
        return (nf + 1 - g) // 2

    def y_range(g):
        return (h0 + 1 - g) // 2, (h1 + 1 - g) // 2

    def send_z():
        top = (nf + 1) // 2
        for d in range(2):

            @pl.when(z_ok[d])
            def _():
                @pl.loop(0, top)
                def _(i):
                    j = top - 1 - i
                    for mine in (True, False):

                        @pl.when(j < z_count(c if mine else other))
                        def _():
                            z_copy(d, j, mine).start()

    send_z()

    @pl.loop(0, HALF)
    def _(j):
        own_copy(j).start()

    for d in range(2):

        @pl.when(y_ok[d])
        def _():
            for mine in (True, False):
                lo, hi = y_range(c if mine else other)

                @pl.loop(lo, hi)
                def _(j):
                    q_copy(d, j, mine).start()

    key_half = lax.broadcasted_iota(jnp.int32, (W, CHIP), 0) // TW
    query_half = lax.broadcasted_iota(jnp.int32, (W, CHIP), 1) % W // TW
    apart = jnp.where(key_half == query_half, 0.0, NEG).astype(jnp.float32)

    def width_bias(j):
        return apart * (1 - jnp.minimum(flags[2 * j + c, 2], 1)).astype(jnp.float32)

    def keys_of(block):
        return block[:, 0].reshape(CHIP, HD)

    def values_of(block):
        return jnp.concatenate([block[0, 1], block[1, 1]], axis=1)

    def queries_of(j, part):
        block = own[j, :, 2] if part == 0 else qn[part - 1, j]
        return block.reshape(CHIP, HD)

    def masked_scores(k, q, bias):
        s = dot(k, q, ((1,), (1,)))
        return (s.reshape(CHIP // W, W, CHIP) + bias[None]).reshape(CHIP, CHIP)

    def first(j, part, k, vt, bias):
        s = masked_scores(k, queries_of(j, part), bias)
        m = jnp.max(s, axis=0, keepdims=True)
        p = jnp.exp2((s - m) * SCALE)
        ml[j, part, 0:1] = m
        ml[j, part, 1:2] = jnp.sum(p, axis=0, keepdims=True)
        acc[j, part] = dot(vt, p.astype(jnp.bfloat16), ((1,), (0,)))

    def more(j, part, k, vt, bias):
        s = masked_scores(k, queries_of(j, part), bias)
        m_old = ml[j, part, 0:1]
        m = jnp.maximum(m_old, jnp.max(s, axis=0, keepdims=True))
        p = jnp.exp2((s - m) * SCALE)
        fade = jnp.exp2((m_old - m) * SCALE)
        ml[j, part, 0:1] = m
        ml[j, part, 1:2] = ml[j, part, 1:2] * fade + jnp.sum(p, axis=0, keepdims=True)
        acc[j, part] = acc[j, part] * fade + dot(vt, p.astype(jnp.bfloat16), ((1,), (0,)))

    def give_back(j):
        for d in range(2):
            m = ml[j, d + 1, 0:1]
            total = ml[j, d + 1, 1:2]
            rs[d, j, 0:HD] = (acc[j, d + 1] * (1.0 / total)).astype(jnp.bfloat16)
            level = m * SCALE + jnp.log2(total)
            a = level.astype(jnp.bfloat16).astype(jnp.float32)
            b = (level - a).astype(jnp.bfloat16).astype(jnp.float32)
            row = lax.broadcasted_iota(jnp.int32, (16, CHIP), 0)
            parts = jnp.where(row == 0, a, jnp.where(row == 1, b, jnp.where(row == 2, level - a - b, 0.0)))
            rs[d, j, HD : HD + 16] = parts.astype(jnp.bfloat16)

            @pl.when(y_ok[d])
            def _():
                ret_copy(d, j).start()

    def in_y(j):
        lo, hi = y_range(c)
        return (j >= lo) & (j < hi)

    def when_y(j, body):
        if h0 == 0 and h1 == HEADS:
            body()
        elif h0 < h1:
            pl.when(in_y(j))(body)

    my_z = z_count(c)

    @pl.loop(0, HALF)
    def _(i):
        j = HALF - 1 - i
        own_load(j).wait()
        own_copy(j).wait_recv()
        bias = width_bias(j)
        k, vt = keys_of(own[j]), values_of(own[j])

        def around():
            for d in range(2):

                @pl.when(y_ok[d])
                def _():
                    for half in range(2):
                        pltpu.make_async_remote_copy(
                            src_ref=qn.at[d, j, half],
                            dst_ref=qn.at[d, j, half],
                            send_sem=q_s.at[d, j, 0],
                            recv_sem=q_r.at[d, j, half],
                            device_id=partner,
                            device_id_type=MESH,
                        ).wait_recv()

            first(j, 1, k, vt, bias)
            first(j, 2, k, vt, bias)

            @pl.when(j >= my_z)
            def _():
                give_back(j)

        first(j, 0, k, vt, bias)
        when_y(j, around)

    @pl.loop(0, my_z)
    def _(i):
        j = my_z - 1 - i
        bias = width_bias(j) + (1 - jnp.minimum(flags[2 * j + c, 0], 1)).astype(jnp.float32) * NEG
        for d in range(2):

            @pl.when(z_ok[d])
            def _():
                for half in range(2):
                    pltpu.make_async_remote_copy(
                        src_ref=nb.at[d, j, half],
                        dst_ref=nb.at[d, j, half],
                        send_sem=z_s.at[d, j, 0],
                        recv_sem=z_r.at[d, j, half],
                        device_id=partner,
                        device_id_type=MESH,
                    ).wait_recv()
                k, vt = keys_of(nb[d, j]), values_of(nb[d, j])
                more(j, 0, k, vt, bias)

                def around():
                    more(j, 1, k, vt, bias)
                    more(j, 2, k, vt, bias)

                when_y(j, around)

        when_y(j, lambda: give_back(j))

    @pl.loop(0, HALF)
    def _(i):
        j = HALF - 1 - i
        low = (1 - jnp.minimum(flags[2 * j + c, 1], 1)).astype(jnp.float32) * NEG
        m = ml[j, 0, 0:1] * SCALE
        total = ml[j, 0, 1:2]

        def finish(o):
            o = o.T.astype(jnp.bfloat16)
            oh[j, 0] = o[:TOK]
            oh[j, 1] = o[TOK:]
            o_copy(j).start()
            o_store(j).start()

        def join():
            top = m + jnp.log2(total)
            levels = []
            for d in range(2):

                @pl.when(y_ok[d])
                def _():
                    ret_copy(1 - d, j).wait_recv()

                level = jnp.sum(rr[d, j, HD : HD + 16].astype(jnp.float32), axis=0, keepdims=True)
                levels.append(level + low + jnp.where(y_ok[d], 0.0, NEG))
            best = jnp.maximum(top, jnp.maximum(levels[0], levels[1]))
            w = jnp.exp2(m - best)
            num = acc[j, 0] * w
            den = total * w
            for d in range(2):
                w = jnp.exp2(levels[d] - best)
                num = num + rr[d, j, 0:HD].astype(jnp.float32) * w
                den = den + w
            finish(num * (1.0 / den))

        def alone():
            finish(acc[j, 0] * (1.0 / total))

        if h0 == 0 and h1 == HEADS:
            join()
        elif h0 == h1:
            alone()
        else:
            pl.when(in_y(j))(join)
            pl.when(jnp.logical_not(in_y(j)))(alone)

    @pl.loop(0, HALF)
    def _(j):
        own_copy(j).wait_send()
        o_copy(j).wait_send()
        o_store(j).wait()
        pltpu.make_async_remote_copy(
            src_ref=out.at[2 * j + other],
            dst_ref=out.at[2 * j + other],
            send_sem=o_s.at[j],
            recv_sem=o_r.at[j],
            device_id=partner,
            device_id_type=MESH,
        ).wait_recv()

    for d in range(2):
        for mine in (True, False):

            @pl.when(z_ok[d])
            def _():
                @pl.loop(0, z_count(c if mine else other))
                def _(j):
                    z_copy(d, j, mine).wait_send()

            @pl.when(y_ok[d])
            def _():
                lo, hi = y_range(c if mine else other)

                @pl.loop(lo, hi)
                def _(j):
                    q_copy(d, j, mine).wait_send()
                    if mine:
                        ret_copy(d, j).wait_send()


def attend(index, n_frame, n_chip_y, packed, flags):
    bf16, f32 = jnp.bfloat16, jnp.float32
    dma = pltpu.SemaphoreType.DMA
    return pl.pallas_call(
        functools.partial(kernel, PLANS[index], n_frame, n_chip_y),
        out_shape=jax.ShapeDtypeStruct((HEADS, TOK, HD), bf16),
        in_specs=[pl.BlockSpec(memory_space=pl.ANY), pl.BlockSpec(memory_space=pltpu.SMEM)],
        out_specs=pl.BlockSpec(memory_space=pl.ANY),
        scratch_shapes=[
            pltpu.VMEM((HALF, 2, 3, TOK, HD), bf16),
            pltpu.VMEM((2, HALF, 2, 2, TOK, HD), bf16),
            pltpu.VMEM((2, HALF, 2, TOK, HD), bf16),
            pltpu.VMEM((HALF, 3, HD, CHIP), f32),
            pltpu.VMEM((HALF, 3, 8, CHIP), f32),
            pltpu.VMEM((2, HALF, HD + 16, CHIP), bf16),
            pltpu.VMEM((2, HALF, HD + 16, CHIP), bf16),
            pltpu.VMEM((HALF, 2, TOK, HD), bf16),
            dma((HALF,)),
            dma((HALF,)),
            dma((HALF,)),
            dma((2, HALF, 2)),
            dma((2, HALF, 2)),
            dma((2, HALF, 2)),
            dma((2, HALF, 2)),
            dma((2, HALF)),
            dma((2, HALF)),
            dma((HALF,)),
            dma((HALF,)),
            dma((HALF,)),
        ],
        compiler_params=pltpu.CompilerParams(
            collective_id=index,
            has_side_effects=True,
            vmem_limit_bytes=32 * 1024 * 1024,
        ),
    )(packed, flags)


def shards(queries, key_value, windows):
    n_frame = lax.axis_size("frame")
    n_chip_y = lax.axis_size("height") // 2
    width = HEADS * HD
    vmem = pl.BlockSpec(memory_space=pltpu.VMEM)
    smem = pl.BlockSpec(memory_space=pltpu.SMEM)
    packed, flags, choice = pl.pallas_call(
        sort_kernel,
        out_shape=(
            jax.ShapeDtypeStruct((HEADS, 3, TOK, HD), jnp.bfloat16),
            jax.ShapeDtypeStruct((HEADS, 4), jnp.int32),
            jax.ShapeDtypeStruct((1,), jnp.int32),
        ),
        in_specs=[vmem, vmem, smem],
        out_specs=(vmem, smem, smem),
    )(queries.reshape(TOK, width), key_value.reshape(2, TOK, width), windows)
    branches = [functools.partial(attend, i, n_frame, n_chip_y) for i in range(len(PLANS))]
    slots = lax.switch(choice[0], branches, packed, flags)
    result = pl.pallas_call(
        place_kernel,
        out_shape=jax.ShapeDtypeStruct((TOK, width), jnp.bfloat16),
        in_specs=[vmem, smem],
        out_specs=vmem,
    )(slots, flags)
    return result.reshape(queries.shape)


def solution(mesh):
    in_specs = (
        P(("cand", "frame"), "height", None, None),
        P(None, ("cand", "frame"), "height", None, None),
        P(),
    )
    out_specs = P(("cand", "frame"), "height", None, None)
    return jax.shard_map(shards, mesh=mesh, in_specs=in_specs, out_specs=out_specs, check_vma=False)
```

time: 289 us -> 46.3 us (0.16)
  the two profiles are of different devices: /device:TPU:1 before, /device:TPU:23 now
where the time goes in v1:
time: 46.3 us; the launch traced here: 46.1 us
  Pallas kernels  43.8 us (95%)
  local copies, waits for them, and re-layouts  1.36 us (3%)
  between operations  0.65 us (1%)
    pallas_call x1, Pallas kernels, attend(): pl.pallas_call(functools.partial(kernel, PLANS[index], n_frame, n_chip_y)...  39.8 us
    pallas_call x1, Pallas kernels, shards(): pl.pallas_call(sort_kernel, out_shape=(jax.ShapeDtypeStruct((HEADS, 3, TO...  2.49 us
    pallas_call x1, Pallas kernels, shards(): pl.pallas_call(place_kernel, out_shape=jax.ShapeDtypeStruct((TOK, width),...  1.49 us
    unnamed x1, local copies, waits for them, and re-layouts  1.36 us

profile of v1, /device:TPU:23, one launch (start us, length us, event | category | flops | bytes accessed | tf_op | source)
XLA Modules:
  0.0 46.1 jit_solution(9179820043053288264)
XLA Ops:
  0.0 1.4 %copy.4.win = s32[12,3]{1,0:T(8,128)} copy(s32[12,3]{0,1:T(4,128)} %param.11) | data formatting | bytes 288 | tf_op args[2]
  1.4 2.5 %shard_map.37 = (bf16[12,3,128,128]{3,2,1,0:T(8,128)(2,1)S(1)}, s32[12,4]{1,0:T(8,128)S(1)}, s32[1]{0:T(128)}) custom-call(bf16[128,1536]{1,0:T(8,128)(2,1)} %bitcast.5, bf16[2,128,1536]{2,1,0:T(8,128)(2,1)} %bitcast.4, s32[12,3]{1,0:T(8,128)} %copy.4.win), custom_call_target="tpu_custom_call" | custom-call | tf_op jit(solution)/shard_map/pallas_call | solution.py:497
  4.5 40.1 %conditional.1 = (bf16[12,128,128]{2,1,0:T(8,128)(2,1)S(1)}) conditional(s32[]{:T(128)} %bitcast.2, (bf16[12,3,128,128]{3,2,1,0:T(8,128)(2,1)S(1)}, s32[12,4]{1,0:T(8,128)S(1)}) %tuple.23, (bf16[12,3,128,128]{3,2,1,0:T(8,128)(2,1)S(1)}, s32[12,4]{1,0:T(8,128)S(1)}) %tuple.23, ...), branch_computations={%region_0.0_spmd, %region_1.0_spmd, %region_2.0_spmd, %region_3.0_... | conditional | bytes 8 | solution.py:508
  4.5 39.8 %branch_2_fun.1 = bf16[12,128,128]{2,1,0:T(8,128)(2,1)S(1)} custom-call(bf16[12,3,128,128]{3,2,1,0:T(8,128)(2,1)S(1)} %get-tuple-element.40.packed, s32[12,4]{1,0:T(8,128)S(1)} %get-tuple-element.41.flags), custom_call_target="tpu_custom_call" | custom-call | tf_op jit(solution)/shard_map/cond/branch_2_fun/pallas_call | solution.py:456
  44.6 1.5 %shard_map.38 = bf16[128,1536]{1,0:T(8,128)(2,1)} custom-call(bf16[12,128,128]{2,1,0:T(8,128)(2,1)S(1)} %get-tuple-element.54.o, s32[12,4]{1,0:T(8,128)S(1)} %get-tuple-element.53.flags), custom_call_target="tpu_custom_call" | custom-call | tf_op jit(solution)/shard_map/pallas_call | solution.py:509
